TPU v7x, 32 devices: a whole 2x2x4 slice. The times are simulated.
32 devices in a mesh: gx: 8 (over z, core), gy: 4 (over y, x).
Axes of the slice: x: 2, y: 2, z: 4, core: 2. Of those that a mesh axis runs over, the one named last changes fastest.
Arguments:
- density: float32 [64, 128, 256], P('gx', 'gy'), may hold values from 0.5 to 2
- energy: float32 [64, 128, 256], P('gx', 'gy'), may hold values from 0.5 to 2
- velocity_x: float32 [64, 128, 256], P('gx', 'gy'), may hold values from -0.5 to 0.5
- velocity_y: float32 [64, 128, 256], P('gx', 'gy'), may hold values from -0.5 to 0.5
- velocity_z: float32 [64, 128, 256], P('gx', 'gy'), may hold values from -0.5 to 0.5
- time_step: float32 [1], replicated, may hold values from 0.1 to 0.2
Outputs:
- new_density: float32 [64, 128, 256], P('gx', 'gy')
- new_energy: float32 [64, 128, 256], P('gx', 'gy')
- new_velocity_x: float32 [64, 128, 256], P('gx', 'gy')
- new_velocity_y: float32 [64, 128, 256], P('gx', 'gy')
- new_velocity_z: float32 [64, 128, 256], P('gx', 'gy')
- next_step: float32 [1], replicated
All inputs are finite; a program needn't handle non-finite values.
Results may differ from a plain program's by a relative error of at most 0.0003.
Values sent between devices are 32-bit elements; how exact they have to be, the bound alone decides.
A program may use at most 64 MiB of HBM per device.

v0:
```python
import jax
import jax.numpy as jnp
from jax import lax
from jax.sharding import PartitionSpec as P


def padded_2(block, sides, width):
    for axis, dim in sides:
        count = lax.axis_size(axis)
        forward = [(i, i + 1) for i in range(count - 1)]
        forward.append((count - 1, 0))
        backward = [(target, source) for source, target in forward]
        low = lax.ppermute(
            lax.slice_in_dim(block, block.shape[dim] - width, None, axis=dim), axis, forward
        )
        high = lax.ppermute(lax.slice_in_dim(block, 0, width, axis=dim), axis, backward)
        block = jnp.concatenate([low, block, high], axis=dim)
    return block


def shifted(field, offset, along):
    return jnp.roll(field, -offset, along)


def van_leer(left_diff, right_diff):
    product = left_diff * right_diff
    agree = product > 0
    return jnp.where(agree, 2.0 * product / jnp.where(agree, left_diff + right_diff, 1.0), 0.0)


def centre(field):
    return field[1:-1, 1:-1]


def diff_x(field):
    return 0.5 * (field[2:, 1:-1] - field[:-2, 1:-1])


def diff_y(field):
    return 0.5 * (field[1:-1, 2:] - field[1:-1, :-2])


def diff_z(field):
    inner = centre(field)
    return 0.5 * (shifted(inner, 1, 2) - shifted(inner, -1, 2))


def lagrange(density, energy, velocity_x, velocity_y, velocity_z, delta_t):
    pressure = 0.4 * density * energy
    diverge = diff_x(velocity_x) + diff_y(velocity_y) + diff_z(velocity_z)
    dens_core = centre(density)
    energy_core = centre(energy)
    press_core = centre(pressure)
    volume = 1.0 + delta_t * diverge
    lag_density = dens_core / volume
    energy_half = energy_core - 0.5 * delta_t * press_core * diverge / dens_core
    press_half = 0.4 * dens_core * energy_half
    lag_energy = energy_core - delta_t * press_half * diverge / dens_core
    new_velx = centre(velocity_x) - delta_t * diff_x(pressure) / dens_core
    new_vely = centre(velocity_y) - delta_t * diff_y(pressure) / dens_core
    new_velz = centre(velocity_z) - delta_t * diff_z(pressure) / dens_core
    return (lag_density, lag_energy, new_velx, new_vely, new_velz)


def sweep_cut(density, mass_energy, velocity, delta_t, along):

    def window(field, lower, upper):
        return lax.slice_in_dim(field, lower, field.shape[along] - upper, axis=along)

    courant = delta_t * (0.5 * (window(velocity, 1, 2) + window(velocity, 2, 1)))
    weight = 0.5 * (1.0 - jnp.abs(courant))

    def face_value(field):
        slope = van_leer(
            window(field, 1, 1) - window(field, 0, 2), window(field, 2, 0) - window(field, 1, 1)
        )
        ahead = window(field, 1, 2) + weight * window(slope, 0, 1)
        behind = window(field, 2, 1) - weight * window(slope, 1, 0)
        return jnp.where(courant > 0, ahead, behind)

    flux = courant * face_value(density)
    energy_flux = courant * face_value(mass_energy)
    dens_out = window(density, 2, 2) + window(flux, 0, 1) - window(flux, 1, 0)
    mass_out = window(mass_energy, 2, 2) + window(energy_flux, 0, 1) - window(energy_flux, 1, 0)
    return (dens_out, mass_out)


def sweep_roll(density, mass_energy, velocity, delta_t, along):
    courant = delta_t * (0.5 * (velocity + shifted(velocity, 1, along)))
    weight = 0.5 * (1.0 - jnp.abs(courant))

    def face_value(field):
        slope = van_leer(field - shifted(field, -1, along), shifted(field, 1, along) - field)
        ahead = field + weight * slope
        behind = shifted(field, 1, along) - weight * shifted(slope, 1, along)
        return jnp.where(courant > 0, ahead, behind)

    flux = courant * face_value(density)
    energy_flux = courant * face_value(mass_energy)
    dens_out = density + shifted(flux, -1, along) - flux
    mass_out = mass_energy + shifted(energy_flux, -1, along) - energy_flux
    return (dens_out, mass_out)


def local(density, energy, velocity_x, velocity_y, velocity_z, time_step):
    delta_t = time_step[0]
    stacked = jnp.stack([density, energy, velocity_x, velocity_y])
    padded = padded_2(stacked, (("gx", 1), ("gy", 2)), 1)
    padded_z = jnp.pad(velocity_z, ((1, 1), (1, 1), (0, 0)))
    lag_density, lag_energy, new_velx, new_vely, new_velz = lagrange(
        padded[0], padded[1], padded[2], padded[3], padded_z, delta_t
    )
    mass_energy = lag_density * lag_energy
    x_padded = padded_2(jnp.stack([lag_density, mass_energy, new_velx]), (("gx", 1),), 2)
    dens_a, mass_a = sweep_cut(x_padded[0], x_padded[1], x_padded[2], delta_t, 0)
    y_padded = padded_2(jnp.stack([dens_a, mass_a, new_vely]), (("gy", 2),), 2)
    dens_b, mass_b = sweep_cut(y_padded[0], y_padded[1], y_padded[2], delta_t, 1)
    dens_c, mass_c = sweep_roll(dens_b, mass_b, new_velz, delta_t, 2)
    new_energy = mass_c / dens_c
    speed = jnp.sqrt(0.56 * new_energy) + jnp.abs(new_velx) + jnp.abs(new_vely) + jnp.abs(new_velz)
    limit = lax.pmin(jnp.min(0.5 / speed), ("gx", "gy"))
    return (dens_c, new_energy, new_velx, new_vely, new_velz, limit.reshape(1))


def solution(mesh):
    return jax.shard_map(
        local,
        mesh=mesh,
        in_specs=(
            P("gx", "gy", None),
            P("gx", "gy", None),
            P("gx", "gy", None),
            P("gx", "gy", None),
            P("gx", "gy", None),
            P(),
        ),
        out_specs=(
            P("gx", "gy", None),
            P("gx", "gy", None),
            P("gx", "gy", None),
            P("gx", "gy", None),
            P("gx", "gy", None),
            P(),
        ),
        check_vma=False,
    )
```

profile of v0, /device:TPU:0, one launch (start us, length us, event | category | flops | bytes accessed | tf_op | source)
XLA Modules:
  0.0 75.6 jit_solution(7579679147600908803)
XLA Ops:
  0.7 1.0 %pad_maximum_fusion.16 = (f32[4,1,32,256]{3,2,1,0:T(8,128)S(1)}, f32[4,1,32,256]{3,2,1,0:T(8,128)S(1)}) fusion(f32[1,8,32,256]{3,2,1,0:T(8,128)} %bitcast.89, f32[1,8,32,256]{3,2,1,0:T(8,128)} %bitcast.92, f32[1,8,32,256]{3,2,1,0:T(8,128)} %bitcast.95, f32[1,8,32,256]{3,2,1,0:T(8,128)} %bitcast.98), kind=kLoop, calls=%fused_computation.138 | loop fusion | flops 196608 | bytes 1310720 | tf_op jit(solution)/shard_map/slice | solution.py:14
  1.7 0.5 collective-permute-start
  2.2 4.1 %collective-permute-start.1 = (f32[4,1,32,256]{3,2,1,0:T(8,128)S(1)}, f32[4,1,32,256]{3,2,1,0:T(8,128)S(1)}, u32[]{:S(2)}, u32[]{:S(2)}) collective-permute-start(f32[4,1,32,256]{3,2,1,0:T(8,128)S(1)} %get-tuple-element.22), channel_id=1, source_target_pairs={{4,0},{8,4},{12,8},{16,12},{20,16},{24,20},{28,24},{0,28},{5,1},{9... | collective-permute-start | bytes 393224 | tf_op jit(solution)/shard_map/ppermute | solution.py:16
  6.4 2.5 %collective-permute-done = f32[4,1,32,256]{3,2,1,0:T(8,128)S(1)} collective-permute-done((f32[4,1,32,256]{3,2,1,0:T(8,128)S(1)}, f32[4,1,32,256]{3,2,1,0:T(8,128)S(1)}, u32[]{:S(2)}, u32[]{:S(2)}) %collective-permute-start) | collective-permute-done | bytes 131104 | tf_op jit(solution)/shard_map/ppermute | solution.py:13
  9.1 2.1 %collective-permute-start.2 = (f32[4,10,1,256]{3,2,1,0:T(1,128)S(1)}, f32[4,10,1,256]{3,2,1,0:T(1,128)S(1)}, u32[]{:S(2)}, u32[]{:S(2)}) collective-permute-start(f32[4,10,1,256]{3,2,1,0:T(1,128)S(1)} %get-tuple-element.19), channel_id=1, source_target_pairs={{0,1},{1,2},{2,3},{3,0},{4,5},{5,6},{6,7},{7,4},{8,9},{9,10},{10,1... | collective-permute-start | bytes 122888 | tf_op jit(solution)/shard_map/ppermute | solution.py:13
  11.1 1.0 %collective-permute-start.3 = (f32[4,10,1,256]{3,2,1,0:T(1,128)S(1)}, f32[4,10,1,256]{3,2,1,0:T(1,128)S(1)}, u32[]{:S(2)}, u32[]{:S(2)}) collective-permute-start(f32[4,10,1,256]{3,2,1,0:T(1,128)S(1)} %get-tuple-element.20), channel_id=1, source_target_pairs={{1,0},{2,1},{3,2},{0,3},{5,4},{6,5},{7,6},{4,7},{9,8},{10,9},{11,1... | collective-permute-start | bytes 122888 | tf_op jit(solution)/shard_map/ppermute | solution.py:16
  12.9 1.3 %collective-permute-done.2 = f32[4,10,1,256]{3,2,1,0:T(1,128)S(1)} collective-permute-done((f32[4,10,1,256]{3,2,1,0:T(1,128)S(1)}, f32[4,10,1,256]{3,2,1,0:T(1,128)S(1)}, u32[]{:S(2)}, u32[]{:S(2)}) %collective-permute-start.2) | collective-permute-done | bytes 40992 | tf_op jit(solution)/shard_map/ppermute | solution.py:13
  14.1 1.6 %collective-permute-done.3 = f32[4,10,1,256]{3,2,1,0:T(1,128)S(1)} collective-permute-done((f32[4,10,1,256]{3,2,1,0:T(1,128)S(1)}, f32[4,10,1,256]{3,2,1,0:T(1,128)S(1)}, u32[]{:S(2)}, u32[]{:S(2)}) %collective-permute-start.3) | collective-permute-done | bytes 40992 | tf_op jit(solution)/shard_map/ppermute | solution.py:16
  16.5 0.3 fusion.54
  17.1 3.4 %collective-permute-start.5 = (f32[3,2,32,256]{3,2,1,0:T(8,128)S(1)}, f32[3,2,32,256]{3,2,1,0:T(8,128)S(1)}, u32[]{:S(2)}, u32[]{:S(2)}) collective-permute-start(f32[3,2,32,256]{3,2,1,0:T(8,128)S(1)} %get-tuple-element.33), channel_id=1, source_target_pairs={{4,0},{8,4},{12,8},{16,12},{20,16},{24,20},{28,24},{0,28},{5,1},{9... | collective-permute-start | bytes 589832 | tf_op jit(solution)/shard_map/ppermute | solution.py:16
  20.6 4.9 %collective-permute-done.4 = f32[3,2,32,256]{3,2,1,0:T(8,128)S(1)} collective-permute-done((f32[3,2,32,256]{3,2,1,0:T(8,128)S(1)}, f32[3,2,32,256]{3,2,1,0:T(8,128)S(1)}, u32[]{:S(2)}, u32[]{:S(2)}) %collective-permute-start.4) | collective-permute-done | bytes 196640 | tf_op jit(solution)/shard_map/ppermute | solution.py:13
  25.5 0.2 pad_maximum_fusion.1
  25.8 0.2 fusion.12
  26.6 2.5 %collective-permute-start.6 = (f32[3,8,2,256]{3,2,1,0:T(2,128)S(1)}, f32[3,8,2,256]{3,2,1,0:T(2,128)S(1)}, u32[]{:S(2)}, u32[]{:S(2)}) collective-permute-start(f32[3,8,2,256]{3,2,1,0:T(2,128)S(1)} %get-tuple-element.29), channel_id=1, source_target_pairs={{0,1},{1,2},{2,3},{3,0},{4,5},{5,6},{6,7},{7,4},{8,9},{9,10},{10,1... | collective-permute-start | bytes 147464 | tf_op jit(solution)/shard_map/ppermute | solution.py:13
  29.1 0.5 collective-permute-start.7
  29.7 1.9 %collective-permute-done.6 = f32[3,8,2,256]{3,2,1,0:T(2,128)S(1)} collective-permute-done((f32[3,8,2,256]{3,2,1,0:T(2,128)S(1)}, f32[3,8,2,256]{3,2,1,0:T(2,128)S(1)}, u32[]{:S(2)}, u32[]{:S(2)}) %collective-permute-start.6) | collective-permute-done | bytes 49184 | tf_op jit(solution)/shard_map/ppermute | solution.py:13
  31.6 1.5 %collective-permute-done.7 = f32[3,8,2,256]{3,2,1,0:T(2,128)S(1)} collective-permute-done((f32[3,8,2,256]{3,2,1,0:T(2,128)S(1)}, f32[3,8,2,256]{3,2,1,0:T(2,128)S(1)}, u32[]{:S(2)}, u32[]{:S(2)}) %collective-permute-start.7) | collective-permute-done | bytes 49184 | tf_op jit(solution)/shard_map/ppermute | solution.py:16
  33.4 0.3 divide_select_fusion
  33.7 0.4 fusion.6
  35.0 0.3 copy-done.4
  35.6 0.6 copy-done.5
  36.3 0.4 fusion.47
  36.9 1.7 %fusion.55 = (f32[]{:T(128)}, f32[8,32,256]{2,1,0:T(8,128)}, f32[8,32,256]{2,1,0:T(8,128)}) fusion(f32[8,32,256]{2,1,0:T(8,128)S(1)} %get-tuple-element.38, f32[8,32,256]{2,1,0:T(8,128)S(1)} %get-tuple-element.27, f32[8,32,256]{2,1,0:T(8,128)S(1)} %get-tuple-element.28, f32[8,32,256]{2,1,0:T(8,128)S(1)} %get-tuple-element.36, ...), kind=kLoop, calls=%fused_computation.129 | loop fusion | flops 1048575 | bytes 2883588 | tf_op jit(solution)/shard_map/reduce_min | solution.py:121
  38.6 37.1 %pmin.7 = f32[1]{0:T(128)} all-reduce(f32[1]{0:T(128)} %bitcast.29), channel_id=1, replica_groups=mesh['gx'=8,'gy'=4] {'gx','gy'}, use_global_device_ids=true, to_apply=%region_1.2 | all-reduce | flops 1 | bytes 8 | tf_op jit(solution)/shard_map/pmin | solution.py:121
  (54 shorter events, 3.6 us)
Async XLA Ops:
  0.6 8.3 %copy-start.9 = (f32[8,32,256]{2,1,0:T(8,128)S(1)}, f32[8,32,256]{2,1,0:T(8,128)}, u32[]{:S(2)}) copy-start(f32[8,32,256]{2,1,0:T(8,128)} %param.6) | copy-start | bytes 786436
  0.6 8.3 %copy-start.8 = (f32[8,32,256]{2,1,0:T(8,128)S(1)}, f32[8,32,256]{2,1,0:T(8,128)}, u32[]{:S(2)}) copy-start(f32[8,32,256]{2,1,0:T(8,128)} %param.7) | copy-start | bytes 786436
  0.7 8.3 %copy-start.7 = (f32[8,32,256]{2,1,0:T(8,128)S(1)}, f32[8,32,256]{2,1,0:T(8,128)}, u32[]{:S(2)}) copy-start(f32[8,32,256]{2,1,0:T(8,128)} %param.8) | copy-start | bytes 786436
  0.7 8.3 %copy-start.6 = (f32[8,32,256]{2,1,0:T(8,128)S(1)}, f32[8,32,256]{2,1,0:T(8,128)}, u32[]{:S(2)}) copy-start(f32[8,32,256]{2,1,0:T(8,128)} %param.9) | copy-start | bytes 786436
  0.7 5.6 %copy-start.3 = (f32[8,32,256]{2,1,0:T(8,128)S(1)}, f32[8,32,256]{2,1,0:T(8,128)}, u32[]{:S(2)}) copy-start(f32[8,32,256]{2,1,0:T(8,128)} %param.10) | copy-start | bytes 786436
  1.7 7.3 %collective-permute-start = (f32[4,1,32,256]{3,2,1,0:T(8,128)S(1)}, f32[4,1,32,256]{3,2,1,0:T(8,128)S(1)}, u32[]{:S(2)}, u32[]{:S(2)}) collective-permute-start(f32[4,1,32,256]{3,2,1,0:T(8,128)S(1)} %get-tuple-element.21), channel_id=1, source_target_pairs={{0,4},{4,8},{8,12},{12,16},{16,20},{20,24},{24,28},{28,0},{1,5},{5... | collective-permute-start | bytes 393224 | tf_op jit(solution)/shard_map/ppermute | solution.py:13
  2.2 6.8 %collective-permute-start.1 = (f32[4,1,32,256]{3,2,1,0:T(8,128)S(1)}, f32[4,1,32,256]{3,2,1,0:T(8,128)S(1)}, u32[]{:S(2)}, u32[]{:S(2)}) collective-permute-start(f32[4,1,32,256]{3,2,1,0:T(8,128)S(1)} %get-tuple-element.22), channel_id=1, source_target_pairs={{4,0},{8,4},{12,8},{16,12},{20,16},{24,20},{28,24},{0,28},{5,1},{9... | collective-permute-start | bytes 393224 | tf_op jit(solution)/shard_map/ppermute | solution.py:16
  9.1 5.1 %collective-permute-start.2 = (f32[4,10,1,256]{3,2,1,0:T(1,128)S(1)}, f32[4,10,1,256]{3,2,1,0:T(1,128)S(1)}, u32[]{:S(2)}, u32[]{:S(2)}) collective-permute-start(f32[4,10,1,256]{3,2,1,0:T(1,128)S(1)} %get-tuple-element.19), channel_id=1, source_target_pairs={{0,1},{1,2},{2,3},{3,0},{4,5},{5,6},{6,7},{7,4},{8,9},{9,10},{10,1... | collective-permute-start | bytes 122888 | tf_op jit(solution)/shard_map/ppermute | solution.py:13
  11.1 4.6 %collective-permute-start.3 = (f32[4,10,1,256]{3,2,1,0:T(1,128)S(1)}, f32[4,10,1,256]{3,2,1,0:T(1,128)S(1)}, u32[]{:S(2)}, u32[]{:S(2)}) collective-permute-start(f32[4,10,1,256]{3,2,1,0:T(1,128)S(1)} %get-tuple-element.20), channel_id=1, source_target_pairs={{1,0},{2,1},{3,2},{0,3},{5,4},{6,5},{7,6},{4,7},{9,8},{10,9},{11,1... | collective-permute-start | bytes 122888 | tf_op jit(solution)/shard_map/ppermute | solution.py:16
  16.9 20.0 %copy-start = (f32[8,32,256]{2,1,0:T(8,128)}, f32[8,32,256]{2,1,0:T(8,128)S(1)}, u32[]{:S(2)}) copy-start(f32[8,32,256]{2,1,0:T(8,128)S(1)} %get-tuple-element.28) | copy-start | bytes 786436
  16.9 20.0 %copy-start.2 = (f32[8,32,256]{2,1,0:T(8,128)}, f32[8,32,256]{2,1,0:T(8,128)S(1)}, u32[]{:S(2)}) copy-start(f32[8,32,256]{2,1,0:T(8,128)S(1)} %get-tuple-element.27) | copy-start | bytes 786436
  16.9 8.6 %collective-permute-start.4 = (f32[3,2,32,256]{3,2,1,0:T(8,128)S(1)}, f32[3,2,32,256]{3,2,1,0:T(8,128)S(1)}, u32[]{:S(2)}, u32[]{:S(2)}) collective-permute-start(f32[3,2,32,256]{3,2,1,0:T(8,128)S(1)} %get-tuple-element.34), channel_id=1, source_target_pairs={{0,4},{4,8},{8,12},{12,16},{16,20},{20,24},{24,28},{28,0},{1,5},{5... | collective-permute-start | bytes 589832 | tf_op jit(solution)/shard_map/ppermute | solution.py:13
  17.1 8.4 %collective-permute-start.5 = (f32[3,2,32,256]{3,2,1,0:T(8,128)S(1)}, f32[3,2,32,256]{3,2,1,0:T(8,128)S(1)}, u32[]{:S(2)}, u32[]{:S(2)}) collective-permute-start(f32[3,2,32,256]{3,2,1,0:T(8,128)S(1)} %get-tuple-element.33), channel_id=1, source_target_pairs={{4,0},{8,4},{12,8},{16,12},{20,16},{24,20},{28,24},{0,28},{5,1},{9... | collective-permute-start | bytes 589832 | tf_op jit(solution)/shard_map/ppermute | solution.py:16
  26.5 10.3 %copy-start.1 = (f32[8,32,256]{2,1,0:T(8,128)}, f32[8,32,256]{2,1,0:T(8,128)S(1)}, u32[]{:S(2)}) copy-start(f32[8,32,256]{2,1,0:T(8,128)S(1)} %get-tuple-element.38) | copy-start | bytes 786436
  26.6 5.0 %collective-permute-start.6 = (f32[3,8,2,256]{3,2,1,0:T(2,128)S(1)}, f32[3,8,2,256]{3,2,1,0:T(2,128)S(1)}, u32[]{:S(2)}, u32[]{:S(2)}) collective-permute-start(f32[3,8,2,256]{3,2,1,0:T(2,128)S(1)} %get-tuple-element.29), channel_id=1, source_target_pairs={{0,1},{1,2},{2,3},{3,0},{4,5},{5,6},{6,7},{7,4},{8,9},{9,10},{10,1... | collective-permute-start | bytes 147464 | tf_op jit(solution)/shard_map/ppermute | solution.py:13
  29.1 4.1 %collective-permute-start.7 = (f32[3,8,2,256]{3,2,1,0:T(2,128)S(1)}, f32[3,8,2,256]{3,2,1,0:T(2,128)S(1)}, u32[]{:S(2)}, u32[]{:S(2)}) collective-permute-start(f32[3,8,2,256]{3,2,1,0:T(2,128)S(1)} %get-tuple-element.30), channel_id=1, source_target_pairs={{1,0},{2,1},{3,2},{0,3},{5,4},{6,5},{7,6},{4,7},{9,8},{10,9},{11,1... | collective-permute-start | bytes 147464 | tf_op jit(solution)/shard_map/ppermute | solution.py:16
  34.6 0.7 copy-start.4
  35.3 0.9 %copy-start.5 = (f32[8,32,256]{2,1,0:T(8,128)S(1)}, f32[8,32,256]{2,1,0:T(8,128)}, u32[]{:S(2)}) copy-start(f32[8,32,256]{2,1,0:T(8,128)} %copy-done.4) | copy-start | bytes 786436
  35.3 1.0 %slice-start = ((f32[8,32,256]{2,1,0:T(8,128)}), f32[8,32,1]{2,1,0:T(8,128)S(1)}, s32[]{:S(2)}) async-start(f32[8,32,256]{2,1,0:T(8,128)} %copy-done.4), calls=%async_computation | async-start | bytes 262144 | tf_op jit(solution)/shard_map/jit(_roll_static)/slice | solution.py:22
where the time goes:
time: 76.7 us; the launch traced here: 75.6 us
  blocking collectives  37.1 us (48%)
  starting transfers between devices  14.3 us (19%)
  waiting for transfers between devices  13.8 us (18%)
  other arithmetic  6.27 us (8%)
  local copies, waits for them, and re-layouts  2.6 us (3%)
  between operations  1.67 us (2%)
    pmin x1, blocking collectives, local(): limit = lax.pmin(jnp.min(0.5 / speed), ('gx', 'gy'))  37.1 us
    ppermute x4, waiting for transfers between devices, padded_2(): lax.ppermute(lax.slice_in_dim(block, block.shape[dim] - width, None, axis...  10.6 us
    ppermute x4, starting transfers between devices, padded_2(): lax.ppermute(lax.slice_in_dim(block, 0, width, axis=dim), axis, backward)  9.05 us
    ppermute x4, starting transfers between devices, padded_2(): lax.ppermute(lax.slice_in_dim(block, block.shape[dim] - width, None, axis...  5.21 us
    ppermute x4, waiting for transfers between devices, padded_2(): lax.ppermute(lax.slice_in_dim(block, 0, width, axis=dim), axis, backward)  3.14 us
    reduce_min x1, other arithmetic, local(): limit = lax.pmin(jnp.min(0.5 / speed), ('gx', 'gy'))  1.7 us
  transfers between devices with their start and end apart: 8, of which 6 were waited for; matrix products, arithmetic and copies ran while one was open for 1% of the time, Pallas kernels for 0%

commit v1 on v0

v1 whole, which is shorter than its diff:
```python
import functools

import jax
import jax.numpy as jnp
from jax import lax
from jax.experimental import pallas as pl
from jax.experimental.pallas import tpu as pltpu
from jax.sharding import PartitionSpec as P

MESH = pl.DeviceIdType.MESH


def limited(left, right):
    product = left * right
    agree = product > 0
    return jnp.where(agree, 2.0 * product / jnp.where(agree, left + right, 1.0), 0.0)


def kernel(
    nx, ny,
    t_ref, d_hbm, e_hbm, vx_hbm, vy_hbm, vz_hbm,
    dens_out, energy_out, nvx_out, nvy_out, nvz_out, limit_out,
    d_s, e_s, xp, vy_s, vz_s, div_s, rate_s,
    a_send, a_lo, a_hi, lm, nvx_h, swept, c_send, c_lo, c_hi,
    top_s, top_x, top_y,
    load_sem, send_sem, recv_sem, x_send, x_recv, y_send, y_recv,
):
    layers, rows, cols = d_s.shape
    ix, iy = lax.axis_index("gx"), lax.axis_index("gy")

    def along_x(step):
        return (lax.rem(ix + step, nx), iy)

    def along_y(step):
        return (ix, lax.rem(iy + step, ny))

    barrier = pltpu.get_barrier_semaphore()
    for step in range(1, nx):
        pl.semaphore_signal(barrier, inc=1, device_id=along_x(step), device_id_type=MESH)
    for step in range(1, ny):
        pl.semaphore_signal(barrier, inc=1, device_id=along_y(step), device_id_type=MESH)

    loads = [
        pltpu.make_async_copy(d_hbm, d_s, load_sem.at[0]),
        pltpu.make_async_copy(e_hbm, e_s, load_sem.at[1]),
        pltpu.make_async_copy(vx_hbm, xp.at[pl.ds(1, layers), 0], load_sem.at[2]),
        pltpu.make_async_copy(vy_hbm, vy_s, load_sem.at[3]),
        pltpu.make_async_copy(vz_hbm, vz_s, load_sem.at[4]),
    ]
    for load in loads:
        load.start()
    t = t_ref[0]

    def remote(src, dst, index, device):
        return pltpu.make_async_remote_copy(
            src_ref=src, dst_ref=dst, send_sem=send_sem.at[index], recv_sem=recv_sem.at[index],
            device_id=device, device_id_type=MESH,
        )

    x_next, x_prev = along_x(1), along_x(nx - 1)
    y_next, y_prev = along_y(1), along_y(ny - 1)

    for load in loads:
        load.wait()

    @pl.loop(0, layers)
    def _(l):
        xp[l + 1, 1] = 0.4 * d_s[l] * e_s[l]

    a_send[0, 0] = vy_s[:, 0, :]
    a_send[0, 1] = xp[1 : layers + 1, 1, 0, :]
    a_send[1, 0] = vy_s[:, rows - 1, :]
    a_send[1, 1] = xp[1 : layers + 1, 1, rows - 1, :]

    pl.semaphore_wait(barrier, nx - 1 + ny - 1)
    first = [
        remote(xp.at[1], xp.at[layers + 1], 0, x_prev),
        remote(xp.at[layers], xp.at[0], 1, x_next),
        remote(a_send.at[0], a_hi, 2, y_prev),
        remote(a_send.at[1], a_lo, 3, y_next),
    ]
    for copy in first:
        copy.start()

    @pl.loop(0, layers)
    def _(l):
        rate = (0.5 * t) / d_s[l]
        vz, p = vz_s[l], xp[l + 1, 1]
        rate_s[l] = rate
        div_s[l] = 0.5 * (pltpu.roll(vz, cols - 1, 1) - pltpu.roll(vz, 1, 1))
        nvz_out[l] = vz - rate * (pltpu.roll(p, cols - 1, 1) - pltpu.roll(p, 1, 1))

    for copy in first:
        copy.wait()

    row = lax.broadcasted_iota(jnp.int32, (rows, cols), 0)

    def lagrange(l):
        def diff_y(f, which):
            ahead = jnp.where(row == rows - 1, a_hi[which, pl.ds(l, 1), :], pltpu.roll(f, rows - 1, 0))
            behind = jnp.where(row == 0, a_lo[which, pl.ds(l, 1), :], pltpu.roll(f, 1, 0))
            return ahead - behind

        rate, vy, energy = rate_s[l], vy_s[l], e_s[l]
        diverge = 0.5 * (xp[l + 2, 0] - xp[l, 0]) + 0.5 * diff_y(vy, 0) + div_s[l]
        td = t * diverge
        half = energy - 0.2 * td * energy
        lag_energy = energy - 0.4 * td * half
        lag_density = d_s[l] / (1.0 + td)
        lm[l + 2, 0] = lag_density
        lm[l + 2, 1] = lag_density * lag_energy
        nvx = xp[l + 1, 0] - rate * (xp[l + 2, 1] - xp[l, 1])
        nvx_h[l + 1] = nvx
        nvx_out[l] = nvx
        nvy_out[l] = vy - rate * diff_y(xp[l + 1, 1], 1)

    @pl.loop(0, 4)
    def _(i):
        lagrange(i + (i // 2) * (layers - 4))

    second = [
        remote(lm.at[pl.ds(2, 2)], lm.at[pl.ds(layers + 2, 2)], 4, x_prev),
        remote(lm.at[pl.ds(layers, 2)], lm.at[pl.ds(0, 2)], 5, x_next),
        remote(nvx_h.at[1], nvx_h.at[layers + 1], 6, x_prev),
        remote(nvx_h.at[layers], nvx_h.at[0], 7, x_next),
    ]
    for copy in second:
        copy.start()

    @pl.loop(2, layers - 2)
    def _(l):
        lagrange(l)

    def sweep_x(lower, upper):
        @pl.loop(0, rows // 8)
        def _(block):
            part = pl.ds(pl.multiple_of(block * 8, 8), 8)

            def slope(f, l):
                return limited(f[l] - f[l - 1], f[l + 1] - f[l])

            courants = {}
            for l in range(lower - 1, upper):
                courants[l] = (0.5 * t) * (nvx_h[l + 1, part] + nvx_h[l + 2, part])
            for field in range(2):
                f = {l: lm[l + 2, field, part] for l in range(lower - 2, upper + 2)}
                here = slope(f, lower - 1)
                flux = None
                for l in range(lower - 1, upper):
                    courant = courants[l]
                    weight = 0.5 - 0.5 * jnp.abs(courant)
                    after = slope(f, l + 1)
                    face = jnp.where(courant > 0, f[l] + weight * here, f[l + 1] - weight * after)
                    now = courant * face
                    if flux is not None:
                        swept[l, field, part] = f[l] + flux - now
                    flux, here = now, after

    if layers > 4:
        sweep_x(2, layers - 2)
    for copy in second:
        copy.wait()
    sweep_x(0, 2)
    sweep_x(layers - 2, layers)

    for side, edge in enumerate((0, rows - 2)):
        for j in range(2):
            for field in range(2):
                c_send[side, 2 * field + j] = swept[:, field, edge + j, :]
        c_send[side, 4] = nvy_out[:, 0 if side == 0 else rows - 1, :]

    third = [
        remote(c_send.at[0], c_hi, 8, y_prev),
        remote(c_send.at[1], c_lo, 9, y_next),
    ]
    for copy in third:
        copy.start()
    for copy in third:
        copy.wait()

    tall = rows + 8
    tile = lax.broadcasted_iota(jnp.int32, (8, cols), 0)

    def sweep(fields, velocity, axis):
        size = velocity.shape[axis]

        def ahead(f):
            return pltpu.roll(f, size - 1, axis)

        def behind(f):
            return pltpu.roll(f, 1, axis)

        courant = (0.5 * t) * (velocity + ahead(velocity))
        weight = 0.5 - 0.5 * jnp.abs(courant)
        out = []
        for f in fields:
            after = ahead(f)
            right = after - f
            slope = limited(behind(right), right)
            flux = courant * jnp.where(courant > 0, f + weight * slope, after - weight * ahead(slope))
            out.append(f + behind(flux) - flux)
        return out

    def finish(l, top):
        def halo(low_first, low_last, high_first, high_last):
            low = jnp.where(tile == 7, c_lo[low_last, pl.ds(l, 1), :], c_lo[low_first, pl.ds(l, 1), :])
            high = jnp.where(tile == 0, c_hi[high_first, pl.ds(l, 1), :], c_hi[high_last, pl.ds(l, 1), :])
            return jnp.where(tile < 4, high, low)

        fields = [
            jnp.concatenate([swept[l, k], halo(2 * k, 2 * k + 1, 2 * k, 2 * k + 1)], axis=0)
            for k in range(2)
        ]
        nvy = nvy_out[l]
        velocity = jnp.concatenate([nvy, halo(4, 4, 4, 4)], axis=0)
        fields = [f[:rows] for f in sweep(fields, velocity, 0)]
        nvz = nvz_out[l]
        density, mass = sweep(fields, nvz, 1)
        energy = mass / density
        dens_out[l] = density
        energy_out[l] = energy
        speed = jnp.sqrt(0.56 * energy) + jnp.abs(nvx_out[l]) + jnp.abs(nvy) + jnp.abs(nvz)
        return jnp.maximum(top, speed)

    top = lax.fori_loop(0, layers, finish, jnp.zeros((rows, cols), jnp.float32))

    def reduced(value):
        return jnp.full((8, 128), jnp.max(value), jnp.float32)

    def share(value, slot, buffer, count, device, sends, recvs):
        top_s[slot] = value
        copies = [
            pltpu.make_async_remote_copy(
                src_ref=top_s.at[slot], dst_ref=buffer.at[step - 1],
                send_sem=sends.at[step - 1], recv_sem=recvs.at[step - 1],
                device_id=device(step), device_id_type=MESH,
            )
            for step in range(1, count)
        ]
        for copy in copies:
            copy.start()
        for copy in copies:
            copy.wait()
        for step in range(1, count):
            value = jnp.maximum(value, buffer[step - 1])
        return value

    best = share(reduced(top), 0, top_x, nx, along_x, x_send, x_recv)
    best = share(best, 1, top_y, ny, along_y, y_send, y_recv)
    limit_out[0] = jnp.max(0.5 / best)


def local(nx, ny, density, energy, velocity_x, velocity_y, velocity_z, time_step):
    layers, rows, cols = density.shape
    full = jax.ShapeDtypeStruct(density.shape, jnp.float32)

    def vmem(*shape):
        return pltpu.VMEM(shape, jnp.float32)

    dma = pltpu.SemaphoreType.DMA
    return pl.pallas_call(
        functools.partial(kernel, nx, ny),
        out_shape=(full,) * 5 + (jax.ShapeDtypeStruct((1,), jnp.float32),),
        in_specs=[pl.BlockSpec(memory_space=pltpu.SMEM)] + [pl.BlockSpec(memory_space=pl.ANY)] * 5,
        out_specs=(pl.BlockSpec(memory_space=pltpu.VMEM),) * 5 + (pl.BlockSpec(memory_space=pltpu.SMEM),),
        scratch_shapes=[
            vmem(layers, rows, cols), vmem(layers, rows, cols),
            vmem(layers + 2, 2, rows, cols),
            vmem(layers, rows, cols), vmem(layers, rows, cols),
            vmem(layers, rows, cols), vmem(layers, rows, cols),
            vmem(2, 2, layers, cols), vmem(2, layers, cols), vmem(2, layers, cols),
            vmem(layers + 4, 2, rows, cols),
            vmem(layers + 2, rows, cols),
            vmem(layers, 2, rows, cols),
            vmem(2, 5, layers, cols), vmem(5, layers, cols), vmem(5, layers, cols),
            vmem(2, 8, 128), vmem(nx - 1, 8, 128), vmem(ny - 1, 8, 128),
            dma((5,)), dma((10,)), dma((10,)),
            dma((nx - 1,)), dma((nx - 1,)), dma((ny - 1,)), dma((ny - 1,)),
        ],
        compiler_params=pltpu.CompilerParams(
            collective_id=0, has_side_effects=True, vmem_limit_bytes=32 * 1024 * 1024
        ),
    )(time_step, density, energy, velocity_x, velocity_y, velocity_z)


def solution(mesh):
    block = P("gx", "gy", None)
    return jax.shard_map(
        functools.partial(local, mesh.shape["gx"], mesh.shape["gy"]),
        mesh=mesh,
        in_specs=(block,) * 5 + (P(),),
        out_specs=(block,) * 5 + (P(),),
        check_vma=False,
    )
```

time: 76.7 us -> 40.1 us (0.52); the launches traced: 75.6 us -> 39.8 us
  blocking collectives: 37.1 us -> 0 us
  Pallas kernels: 0 us -> 28.6 us
  starting transfers between devices: 14.3 us -> 0 us
  waiting for transfers between devices: 13.8 us -> 0 us
  other arithmetic: 6.27 us -> 0 us
  local copies, waits for them, and re-layouts: 2.6 us -> 8.25 us
  between operations: 1.67 us -> 2.99 us
    pmin x1 -> x0, blocking collectives: 37.1 us -> none  [local(): limit = lax.pmin(jnp.min(0.5 / speed), ('gx', 'gy'))]
    pallas_call x0 -> x1, Pallas kernels: none -> 28.6 us  [local(): pl.pallas_call(functools.partial(kernel, nx, ny), out_shape=(full,) * 5 +...]
    ppermute x8 -> x0, starting transfers between devices: 14.3 us -> none  [the longest x4 9.05 us: padded_2(): lax.ppermute(lax.slice_in_dim(block, 0, width, axis=dim), axis, backward)]
    ppermute x8 -> x0, waiting for transfers between devices: 13.8 us -> none  [the longest x4 10.6 us: padded_2(): lax.ppermute(lax.slice_in_dim(block, block.shape[dim] - width, None, axis...]
    unnamed x20 -> x15, local copies, waits for them, and re-layouts: 0.91 us -> 8.25 us
    reduce_min x1 -> x0, other arithmetic: 1.7 us -> none  [local(): limit = lax.pmin(jnp.min(0.5 / speed), ('gx', 'gy'))]
    slice x17 -> x0, local copies, waits for them, and re-layouts: 1.52 us -> none  [shifted(): return jnp.roll(field, -offset, along)]
    mul x5 -> x0, other arithmetic: 1.35 us -> none  [the longest x2 0.59 us: sweep_cut(): flux = courant * face_value(density)]
  transfers between devices with their start and end apart: 8 -> 0, of which waited for: 6 -> 0; matrix products, arithmetic and copies ran while one was open for 1% -> 0% of each run, Pallas kernels for 0% -> 0%
where the time goes in v1:
time: 40.1 us; the launch traced here: 39.8 us
  Pallas kernels  28.6 us (71%)
  local copies, waits for them, and re-layouts  8.25 us (21%)
  between operations  2.99 us (7%)
    pallas_call x1, Pallas kernels, local(): pl.pallas_call(functools.partial(kernel, nx, ny), out_shape=(full,) * 5 +...  28.6 us
    unnamed x15, local copies, waits for them, and re-layouts  8.25 us

profile of v1, /device:TPU:0, one launch (start us, length us, event | category | flops | bytes accessed | tf_op | source)
XLA Modules:
  0.0 39.8 jit_solution(805165400807289070)
XLA Ops:
  1.3 0.0 copy-start
  1.3 0.9 %copy-done = f32[8,32,256]{2,1,0:T(8,128)S(1)} copy-done((f32[8,32,256]{2,1,0:T(8,128)S(1)}, f32[8,32,256]{2,1,0:T(8,128)}, u32[]{:S(2)}) %copy-start) | copy-done | bytes 262168
  2.2 0.0 copy-start.1
  2.2 0.9 %copy-done.1 = f32[8,32,256]{2,1,0:T(8,128)S(1)} copy-done((f32[8,32,256]{2,1,0:T(8,128)S(1)}, f32[8,32,256]{2,1,0:T(8,128)}, u32[]{:S(2)}) %copy-start.1) | copy-done | bytes 262168
  3.2 0.0 copy-start.2
  3.2 0.9 %copy-done.2 = f32[8,32,256]{2,1,0:T(8,128)S(1)} copy-done((f32[8,32,256]{2,1,0:T(8,128)S(1)}, f32[8,32,256]{2,1,0:T(8,128)}, u32[]{:S(2)}) %copy-start.2) | copy-done | bytes 262168
  4.1 0.0 copy-start.3
  4.1 0.9 %copy-done.3 = f32[8,32,256]{2,1,0:T(8,128)S(1)} copy-done((f32[8,32,256]{2,1,0:T(8,128)S(1)}, f32[8,32,256]{2,1,0:T(8,128)}, u32[]{:S(2)}) %copy-start.3) | copy-done | bytes 262168
  5.1 0.0 copy-start.4
  5.1 0.9 %copy-done.4 = f32[8,32,256]{2,1,0:T(8,128)S(1)} copy-done((f32[8,32,256]{2,1,0:T(8,128)S(1)}, f32[8,32,256]{2,1,0:T(8,128)}, u32[]{:S(2)}) %copy-start.4) | copy-done | bytes 262168
  6.0 28.6 %shard_map.109 = (f32[8,32,256]{2,1,0:T(8,128)S(1)}, f32[8,32,256]{2,1,0:T(8,128)S(1)}, f32[8,32,256]{2,1,0:T(8,128)S(1)}, f32[8,32,256]{2,1,0:T(8,128)S(1)}, f32[8,32,256]{2,1,0:T(8,128)S(1)}, /*index=5*/f32[1]{0:T(128)}) custom-call(f32[1]{0:T(128)S(6)} %copy.18.t_ref, f32[8,32,256]{2,1,0:T(8,128)S(1)} %copy-done, f32[8,32,256]{2,1,0:T(8,128)S(1)} %copy-done.1, ...), custom_call_target="tpu_custom_call" | custom-call | tf_op jit(solution)/shard_map/pallas_call | solution.py:261
  34.6 0.7 %copy.19 = f32[8,32,256]{2,1,0:T(8,128)} copy(f32[8,32,256]{2,1,0:T(8,128)S(1)} %get-tuple-element.12) | data formatting | bytes 524288
  35.3 0.7 %copy.20 = f32[8,32,256]{2,1,0:T(8,128)} copy(f32[8,32,256]{2,1,0:T(8,128)S(1)} %get-tuple-element.13) | data formatting | bytes 524288
  36.0 0.7 %copy.21 = f32[8,32,256]{2,1,0:T(8,128)} copy(f32[8,32,256]{2,1,0:T(8,128)S(1)} %get-tuple-element.14) | data formatting | bytes 524288
  36.7 0.7 %copy.22 = f32[8,32,256]{2,1,0:T(8,128)} copy(f32[8,32,256]{2,1,0:T(8,128)S(1)} %get-tuple-element.15) | data formatting | bytes 524288
  37.4 0.7 %copy.23 = f32[8,32,256]{2,1,0:T(8,128)} copy(f32[8,32,256]{2,1,0:T(8,128)S(1)} %get-tuple-element.16) | data formatting | bytes 524288
Async XLA Ops:
  1.3 1.0 %copy-start = (f32[8,32,256]{2,1,0:T(8,128)S(1)}, f32[8,32,256]{2,1,0:T(8,128)}, u32[]{:S(2)}) copy-start(f32[8,32,256]{2,1,0:T(8,128)} %d_hbm.1) | copy-start | bytes 786436
  2.2 0.9 %copy-start.1 = (f32[8,32,256]{2,1,0:T(8,128)S(1)}, f32[8,32,256]{2,1,0:T(8,128)}, u32[]{:S(2)}) copy-start(f32[8,32,256]{2,1,0:T(8,128)} %e_hbm.1) | copy-start | bytes 786436
  3.2 0.9 %copy-start.2 = (f32[8,32,256]{2,1,0:T(8,128)S(1)}, f32[8,32,256]{2,1,0:T(8,128)}, u32[]{:S(2)}) copy-start(f32[8,32,256]{2,1,0:T(8,128)} %vx_hbm.1) | copy-start | bytes 786436
  4.1 0.9 %copy-start.3 = (f32[8,32,256]{2,1,0:T(8,128)S(1)}, f32[8,32,256]{2,1,0:T(8,128)}, u32[]{:S(2)}) copy-start(f32[8,32,256]{2,1,0:T(8,128)} %vy_hbm.1) | copy-start | bytes 786436
  5.1 0.9 %copy-start.4 = (f32[8,32,256]{2,1,0:T(8,128)S(1)}, f32[8,32,256]{2,1,0:T(8,128)}, u32[]{:S(2)}) copy-start(f32[8,32,256]{2,1,0:T(8,128)} %vz_hbm.1) | copy-start | bytes 786436

commit v2 on v1

--- a/solution.py
+++ b/solution.py
@@ -10,10 +10,31 @@
 MESH = pl.DeviceIdType.MESH
 
 
+def inverse(value):
+    guess = pl.reciprocal(value, approx=True)
+    return guess * (2.0 - value * guess)
+
+
 def limited(left, right):
     product = left * right
-    agree = product > 0
-    return jnp.where(agree, 2.0 * product / jnp.where(agree, left + right, 1.0), 0.0)
+    return jnp.maximum(product, 0.0) * inverse(jnp.where(product > 0, left + right, 1.0))
+
+
+def upwind(courant):
+    positive = courant > 0
+    return positive, jnp.where(positive, 1.0, -1.0) - courant
+
+
+def store(*refs):
+    sources, targets, sem = refs[:5], refs[5:10], refs[10]
+    copies = [
+        pltpu.make_async_copy(source, target, sem.at[k])
+        for k, (source, target) in enumerate(zip(sources, targets))
+    ]
+    for copy in copies:
+        copy.start()
+    for copy in copies:
+        copy.wait()
 
 
 def kernel(
@@ -21,7 +42,7 @@
     t_ref, d_hbm, e_hbm, vx_hbm, vy_hbm, vz_hbm,
     dens_out, energy_out, nvx_out, nvy_out, nvz_out, limit_out,
     d_s, e_s, xp, vy_s, vz_s, div_s, rate_s,
-    a_send, a_lo, a_hi, lm, nvx_h, swept, c_send, c_lo, c_hi,
+    a_send, a_lo, a_hi, lm, nvx_h, swept, m_send, m_lo, m_hi, o_send, o_lo, o_hi,
     top_s, top_x, top_y,
     load_sem, send_sem, recv_sem, x_send, x_recv, y_send, y_recv,
 ):
@@ -84,7 +105,7 @@
 
     @pl.loop(0, layers)
     def _(l):
-        rate = (0.5 * t) / d_s[l]
+        rate = (0.5 * t) * inverse(d_s[l])
         vz, p = vz_s[l], xp[l + 1, 1]
         rate_s[l] = rate
         div_s[l] = 0.5 * (pltpu.roll(vz, cols - 1, 1) - pltpu.roll(vz, 1, 1))
@@ -106,7 +127,7 @@
         td = t * diverge
         half = energy - 0.2 * td * energy
         lag_energy = energy - 0.4 * td * half
-        lag_density = d_s[l] / (1.0 + td)
+        lag_density = d_s[l] * inverse(1.0 + td)
         lm[l + 2, 0] = lag_density
         lm[l + 2, 1] = lag_density * lag_energy
         nvx = xp[l + 1, 0] - rate * (xp[l + 2, 1] - xp[l, 1])
@@ -141,44 +162,51 @@
 
             courants = {}
             for l in range(lower - 1, upper):
-                courants[l] = (0.5 * t) * (nvx_h[l + 1, part] + nvx_h[l + 2, part])
+                courant = (0.5 * t) * (nvx_h[l + 1, part] + nvx_h[l + 2, part])
+                courants[l] = (courant,) + upwind(courant)
             for field in range(2):
                 f = {l: lm[l + 2, field, part] for l in range(lower - 2, upper + 2)}
                 here = slope(f, lower - 1)
                 flux = None
                 for l in range(lower - 1, upper):
-                    courant = courants[l]
-                    weight = 0.5 - 0.5 * jnp.abs(courant)
+                    courant, positive, weight = courants[l]
                     after = slope(f, l + 1)
-                    face = jnp.where(courant > 0, f[l] + weight * here, f[l + 1] - weight * after)
+                    face = jnp.where(positive, f[l], f[l + 1]) + weight * jnp.where(positive, here, after)
                     now = courant * face
                     if flux is not None:
                         swept[l, field, part] = f[l] + flux - now
                     flux, here = now, after
 
-    if layers > 4:
-        sweep_x(2, layers - 2)
+    def pack(buffer, parts):
+        for side, edge in enumerate((0, rows - 2)):
+            for first_row, part in parts:
+                to = pl.ds(first_row, part.stop - part.start)
+                for j in range(2):
+                    for field in range(2):
+                        buffer[side, 2 * field + j, to] = swept[part, field, edge + j, :]
+                buffer[side, 4, to] = nvy_out[part, 0 if side == 0 else rows - 1, :]
+
+    def send_rows(buffer, low, high, index):
+        copies = [
+            remote(buffer.at[0], high, index, y_prev),
+            remote(buffer.at[1], low, index + 1, y_next),
+        ]
+        for copy in copies:
+            copy.start()
+        return copies
+
+    sweep_x(2, layers - 2)
+    pack(m_send, [(0, slice(2, layers - 2))])
+    middle = send_rows(m_send, m_lo, m_hi, 8)
     for copy in second:
         copy.wait()
     sweep_x(0, 2)
     sweep_x(layers - 2, layers)
-
-    for side, edge in enumerate((0, rows - 2)):
-        for j in range(2):
-            for field in range(2):
-                c_send[side, 2 * field + j] = swept[:, field, edge + j, :]
-        c_send[side, 4] = nvy_out[:, 0 if side == 0 else rows - 1, :]
-
-    third = [
-        remote(c_send.at[0], c_hi, 8, y_prev),
-        remote(c_send.at[1], c_lo, 9, y_next),
-    ]
-    for copy in third:
-        copy.start()
-    for copy in third:
-        copy.wait()
-
-    tall = rows + 8
+    pack(o_send, [(0, slice(0, 2)), (2, slice(layers - 2, layers))])
+    outer = send_rows(o_send, o_lo, o_hi, 10)
+    for copy in middle:
+        copy.wait()
+
     tile = lax.broadcasted_iota(jnp.int32, (8, cols), 0)
 
     def sweep(fields, velocity, axis):
@@ -191,20 +219,21 @@
             return pltpu.roll(f, 1, axis)
 
         courant = (0.5 * t) * (velocity + ahead(velocity))
-        weight = 0.5 - 0.5 * jnp.abs(courant)
+        positive, weight = upwind(courant)
         out = []
         for f in fields:
             after = ahead(f)
             right = after - f
             slope = limited(behind(right), right)
-            flux = courant * jnp.where(courant > 0, f + weight * slope, after - weight * ahead(slope))
+            face = jnp.where(positive, f, after) + weight * jnp.where(positive, slope, ahead(slope))
+            flux = courant * face
             out.append(f + behind(flux) - flux)
         return out
 
-    def finish(l, top):
+    def finish(l, place, c_lo, c_hi, top):
         def halo(low_first, low_last, high_first, high_last):
-            low = jnp.where(tile == 7, c_lo[low_last, pl.ds(l, 1), :], c_lo[low_first, pl.ds(l, 1), :])
-            high = jnp.where(tile == 0, c_hi[high_first, pl.ds(l, 1), :], c_hi[high_last, pl.ds(l, 1), :])
+            low = jnp.where(tile == 7, c_lo[low_last, pl.ds(place, 1), :], c_lo[low_first, pl.ds(place, 1), :])
+            high = jnp.where(tile == 0, c_hi[high_first, pl.ds(place, 1), :], c_hi[high_last, pl.ds(place, 1), :])
             return jnp.where(tile < 4, high, low)
 
         fields = [
@@ -216,13 +245,20 @@
         fields = [f[:rows] for f in sweep(fields, velocity, 0)]
         nvz = nvz_out[l]
         density, mass = sweep(fields, nvz, 1)
-        energy = mass / density
+        energy = mass * inverse(density)
         dens_out[l] = density
         energy_out[l] = energy
         speed = jnp.sqrt(0.56 * energy) + jnp.abs(nvx_out[l]) + jnp.abs(nvy) + jnp.abs(nvz)
         return jnp.maximum(top, speed)
 
-    top = lax.fori_loop(0, layers, finish, jnp.zeros((rows, cols), jnp.float32))
+    top = lax.fori_loop(
+        0, layers - 4, lambda i, top: finish(i + 2, i, m_lo, m_hi, top), jnp.zeros((rows, cols), jnp.float32)
+    )
+    for copy in outer:
+        copy.wait()
+    top = lax.fori_loop(
+        0, 4, lambda i, top: finish(i + (i // 2) * (layers - 4), i, o_lo, o_hi, top), top
+    )
 
     def reduced(value):
         return jnp.full((8, 128), jnp.max(value), jnp.float32)
@@ -258,10 +294,10 @@
         return pltpu.VMEM(shape, jnp.float32)
 
     dma = pltpu.SemaphoreType.DMA
-    return pl.pallas_call(
+    results = pl.pallas_call(
         functools.partial(kernel, nx, ny),
         out_shape=(full,) * 5 + (jax.ShapeDtypeStruct((1,), jnp.float32),),
-        in_specs=[pl.BlockSpec(memory_space=pltpu.SMEM)] + [pl.BlockSpec(memory_space=pl.ANY)] * 5,
+        in_specs=[pl.BlockSpec(memory_space=pltpu.SMEM)] + [pl.BlockSpec(memory_space=pltpu.HBM)] * 5,
         out_specs=(pl.BlockSpec(memory_space=pltpu.VMEM),) * 5 + (pl.BlockSpec(memory_space=pltpu.SMEM),),
         scratch_shapes=[
             vmem(layers, rows, cols), vmem(layers, rows, cols),
@@ -272,15 +308,24 @@
             vmem(layers + 4, 2, rows, cols),
             vmem(layers + 2, rows, cols),
             vmem(layers, 2, rows, cols),
-            vmem(2, 5, layers, cols), vmem(5, layers, cols), vmem(5, layers, cols),
+            vmem(2, 5, layers - 4, cols), vmem(5, layers - 4, cols), vmem(5, layers - 4, cols),
+            vmem(2, 5, 4, cols), vmem(5, 4, cols), vmem(5, 4, cols),
             vmem(2, 8, 128), vmem(nx - 1, 8, 128), vmem(ny - 1, 8, 128),
-            dma((5,)), dma((10,)), dma((10,)),
+            dma((5,)), dma((12,)), dma((12,)),
             dma((nx - 1,)), dma((nx - 1,)), dma((ny - 1,)), dma((ny - 1,)),
         ],
         compiler_params=pltpu.CompilerParams(
             collective_id=0, has_side_effects=True, vmem_limit_bytes=32 * 1024 * 1024
         ),
-    )(time_step, density, energy, velocity_x, velocity_y, velocity_z)
+    )(time_step, *(pltpu.with_memory_space_constraint(f, pltpu.HBM) for f in (density, energy, velocity_x, velocity_y, velocity_z)))
+    stored = pl.pallas_call(
+        store,
+        out_shape=(full,) * 5,
+        in_specs=[pl.BlockSpec(memory_space=pl.ANY)] * 5,
+        out_specs=(pl.BlockSpec(memory_space=pltpu.HBM),) * 5,
+        scratch_shapes=[dma((5,))],
+    )(*results[:5])
+    return (*stored, results[5])
 
 
 def solution(mesh):

time: 40.1 us -> 74.3 us (1.85)
  Pallas kernels: 28.6 us -> 67.5 us
  local copies, waits for them, and re-layouts: 8.25 us -> 3.5 us
    pallas_call x0 -> x1, Pallas kernels: none -> 40.8 us  [local(): pl.pallas_call(store, out_shape=(full,) * 5, in_specs=[pl.BlockSpec(memor...]
    unnamed x15 -> x10, local copies, waits for them, and re-layouts: 8.25 us -> 3.5 us
    pallas_call x1, Pallas kernels: 28.6 us -> 26.7 us  [local(): pl.pallas_call(functools.partial(kernel, nx, ny), out_shape=(full,) * 5 +...]
where the time goes in v2:
time: 74.3 us; the launch traced here: 74.1 us
  Pallas kernels  67.5 us (91%)
  local copies, waits for them, and re-layouts  3.5 us (5%)
  between operations  3.1 us (4%)
    pallas_call x1, Pallas kernels, local(): pl.pallas_call(store, out_shape=(full,) * 5, in_specs=[pl.BlockSpec(memor...  40.8 us
    pallas_call x1, Pallas kernels, local(): pl.pallas_call(functools.partial(kernel, nx, ny), out_shape=(full,) * 5 +...  26.7 us
    unnamed x10, local copies, waits for them, and re-layouts  3.5 us

profile of v2, /device:TPU:0, one launch (start us, length us, event | category | flops | bytes accessed | tf_op | source)
XLA Modules:
  0.0 74.1 jit_solution(17540975683971008778)
XLA Ops:
  1.3 26.7 %shard_map.109 = (f32[8,32,256]{2,1,0:T(8,128)S(1)}, f32[8,32,256]{2,1,0:T(8,128)S(1)}, f32[8,32,256]{2,1,0:T(8,128)S(1)}, f32[8,32,256]{2,1,0:T(8,128)S(1)}, f32[8,32,256]{2,1,0:T(8,128)S(1)}, /*index=5*/f32[1]{0:T(128)}) custom-call(f32[1]{0:T(128)S(6)} %copy.13.t_ref, f32[8,32,256]{2,1,0:T(8,128)} %d_hbm.1, f32[8,32,256]{2,1,0:T(8,128)} %e_hbm.1, ...), custom_call_target="tpu_custom_call" | custom-call | tf_op jit(solution)/shard_map/pallas_call | solution.py:297
  28.0 0.0 copy-start
  28.0 0.7 copy-done
  28.7 0.0 copy-start.1
  28.7 0.7 copy-done.1
  29.4 0.0 copy-start.2
  29.4 0.7 copy-done.2
  30.1 0.0 copy-start.3
  30.1 0.7 copy-done.3
  30.8 0.0 copy-start.4
  30.8 0.7 copy-done.4
  31.5 40.8 %shard_map.110 = (f32[8,32,256]{2,1,0:T(8,128)}, f32[8,32,256]{2,1,0:T(8,128)}, f32[8,32,256]{2,1,0:T(8,128)}, f32[8,32,256]{2,1,0:T(8,128)}, f32[8,32,256]{2,1,0:T(8,128)}) custom-call(f32[8,32,256]{2,1,0:T(8,128)} %copy-done, f32[8,32,256]{2,1,0:T(8,128)} %copy-done.1, f32[8,32,256]{2,1,0:T(8,128)} %copy-done.2, f32[8,32,256]{2,1,0:T(8,128)} %copy-done.3, ...), custom_call_target="tpu_custom_call" | custom-call | tf_op jit(solution)/shard_map/pallas_call | solution.py:321
Async XLA Ops:
  28.0 0.7 copy-start
  28.7 0.7 copy-start.1
  29.4 0.7 copy-start.2
  30.1 0.7 copy-start.3
  30.8 0.7 copy-start.4

commit v3 on v2

--- a/solution.py
+++ b/solution.py
@@ -27,9 +27,13 @@
 
 def store(*refs):
     sources, targets, sem = refs[:5], refs[5:10], refs[10]
+    layers = sources[0].shape[0]
+    middle = layers // 2
+    parts = (pl.ds(0, middle), pl.ds(middle, layers - middle))
     copies = [
-        pltpu.make_async_copy(source, target, sem.at[k])
+        pltpu.make_async_copy(source.at[part], target.at[part], sem.at[k, side])
         for k, (source, target) in enumerate(zip(sources, targets))
+        for side, part in enumerate(parts)
     ]
     for copy in copies:
         copy.start()
@@ -81,13 +85,15 @@
     x_next, x_prev = along_x(1), along_x(nx - 1)
     y_next, y_prev = along_y(1), along_y(ny - 1)
 
-    for load in loads:
+    for load in loads[:2]:
         load.wait()
 
     @pl.loop(0, layers)
     def _(l):
         xp[l + 1, 1] = 0.4 * d_s[l] * e_s[l]
 
+    for load in loads[2:4]:
+        load.wait()
     a_send[0, 0] = vy_s[:, 0, :]
     a_send[0, 1] = xp[1 : layers + 1, 1, 0, :]
     a_send[1, 0] = vy_s[:, rows - 1, :]
@@ -102,6 +108,7 @@
     ]
     for copy in first:
         copy.start()
+    loads[4].wait()
 
     @pl.loop(0, layers)
     def _(l):
@@ -321,9 +328,9 @@
     stored = pl.pallas_call(
         store,
         out_shape=(full,) * 5,
-        in_specs=[pl.BlockSpec(memory_space=pl.ANY)] * 5,
+        in_specs=[pl.BlockSpec(memory_space=pltpu.VMEM)] * 5,
         out_specs=(pl.BlockSpec(memory_space=pltpu.HBM),) * 5,
-        scratch_shapes=[dma((5,))],
+        scratch_shapes=[dma((5, 2))],
     )(*results[:5])
     return (*stored, results[5])
 

time: 74.3 us -> 35.9 us (0.48)
  Pallas kernels: 67.5 us -> 29.1 us
    pallas_call x1, Pallas kernels: 40.8 us -> 2.39 us  [local(): pl.pallas_call(store, out_shape=(full,) * 5, in_specs=[pl.BlockSpec(memor...]
where the time goes in v3:
time: 35.9 us; the launch traced here: 35.7 us
  Pallas kernels  29.1 us (81%)
  local copies, waits for them, and re-layouts  3.5 us (10%)
  between operations  3.1 us (9%)
    pallas_call x1, Pallas kernels, local(): pl.pallas_call(functools.partial(kernel, nx, ny), out_shape=(full,) * 5 +...  26.7 us
    unnamed x10, local copies, waits for them, and re-layouts  3.5 us
    pallas_call x1, Pallas kernels, local(): pl.pallas_call(store, out_shape=(full,) * 5, in_specs=[pl.BlockSpec(memor...  2.39 us

profile of v3, /device:TPU:0, one launch (start us, length us, event | category | flops | bytes accessed | tf_op | source)
XLA Modules:
  0.0 35.7 jit_solution(5390043950346476038)
XLA Ops:
  1.3 26.7 %shard_map.109 = (f32[8,32,256]{2,1,0:T(8,128)S(1)}, f32[8,32,256]{2,1,0:T(8,128)S(1)}, f32[8,32,256]{2,1,0:T(8,128)S(1)}, f32[8,32,256]{2,1,0:T(8,128)S(1)}, f32[8,32,256]{2,1,0:T(8,128)S(1)}, /*index=5*/f32[1]{0:T(128)}) custom-call(f32[1]{0:T(128)S(6)} %copy.13.t_ref, f32[8,32,256]{2,1,0:T(8,128)} %d_hbm.1, f32[8,32,256]{2,1,0:T(8,128)} %e_hbm.1, ...), custom_call_target="tpu_custom_call" | custom-call | tf_op jit(solution)/shard_map/pallas_call | solution.py:304
  28.0 0.0 copy-start
  28.0 0.7 %copy-done = f32[8,32,256]{2,1,0:T(8,128)} copy-done((f32[8,32,256]{2,1,0:T(8,128)}, f32[8,32,256]{2,1,0:T(8,128)S(1)}, u32[]{:S(2)}) %copy-start) | copy-done | bytes 262168
  28.7 0.0 copy-start.1
  28.7 0.7 %copy-done.1 = f32[8,32,256]{2,1,0:T(8,128)} copy-done((f32[8,32,256]{2,1,0:T(8,128)}, f32[8,32,256]{2,1,0:T(8,128)S(1)}, u32[]{:S(2)}) %copy-start.1) | copy-done | bytes 262168
  29.4 0.0 copy-start.2
  29.4 0.7 %copy-done.2 = f32[8,32,256]{2,1,0:T(8,128)} copy-done((f32[8,32,256]{2,1,0:T(8,128)}, f32[8,32,256]{2,1,0:T(8,128)S(1)}, u32[]{:S(2)}) %copy-start.2) | copy-done | bytes 262168
  30.1 0.0 copy-start.3
  30.1 0.7 %copy-done.3 = f32[8,32,256]{2,1,0:T(8,128)} copy-done((f32[8,32,256]{2,1,0:T(8,128)}, f32[8,32,256]{2,1,0:T(8,128)S(1)}, u32[]{:S(2)}) %copy-start.3) | copy-done | bytes 262168
  30.8 0.0 copy-start.4
  30.8 0.7 %copy-done.4 = f32[8,32,256]{2,1,0:T(8,128)} copy-done((f32[8,32,256]{2,1,0:T(8,128)}, f32[8,32,256]{2,1,0:T(8,128)S(1)}, u32[]{:S(2)}) %copy-start.4) | copy-done | bytes 262168
  31.5 2.4 %shard_map.110 = (f32[8,32,256]{2,1,0:T(8,128)}, f32[8,32,256]{2,1,0:T(8,128)}, f32[8,32,256]{2,1,0:T(8,128)}, f32[8,32,256]{2,1,0:T(8,128)}, f32[8,32,256]{2,1,0:T(8,128)}) custom-call(f32[8,32,256]{2,1,0:T(8,128)} %copy-done, f32[8,32,256]{2,1,0:T(8,128)} %copy-done.1, f32[8,32,256]{2,1,0:T(8,128)} %copy-done.2, f32[8,32,256]{2,1,0:T(8,128)} %copy-done.3, ...), custom_call_target="tpu_custom_call" | custom-call | tf_op jit(solution)/shard_map/pallas_call | solution.py:328
Async XLA Ops:
  28.0 0.7 %copy-start = (f32[8,32,256]{2,1,0:T(8,128)}, f32[8,32,256]{2,1,0:T(8,128)S(1)}, u32[]{:S(2)}) copy-start(f32[8,32,256]{2,1,0:T(8,128)S(1)} %get-tuple-element.17.refs_0_) | copy-start | bytes 786436
  28.7 0.7 %copy-start.1 = (f32[8,32,256]{2,1,0:T(8,128)}, f32[8,32,256]{2,1,0:T(8,128)S(1)}, u32[]{:S(2)}) copy-start(f32[8,32,256]{2,1,0:T(8,128)S(1)} %get-tuple-element.18.refs_1_) | copy-start | bytes 786436
  29.4 0.7 %copy-start.2 = (f32[8,32,256]{2,1,0:T(8,128)}, f32[8,32,256]{2,1,0:T(8,128)S(1)}, u32[]{:S(2)}) copy-start(f32[8,32,256]{2,1,0:T(8,128)S(1)} %get-tuple-element.19.refs_2_) | copy-start | bytes 786436
  30.1 0.7 %copy-start.3 = (f32[8,32,256]{2,1,0:T(8,128)}, f32[8,32,256]{2,1,0:T(8,128)S(1)}, u32[]{:S(2)}) copy-start(f32[8,32,256]{2,1,0:T(8,128)S(1)} %get-tuple-element.20.refs_3_) | copy-start | bytes 786436
  30.8 0.7 %copy-start.4 = (f32[8,32,256]{2,1,0:T(8,128)}, f32[8,32,256]{2,1,0:T(8,128)S(1)}, u32[]{:S(2)}) copy-start(f32[8,32,256]{2,1,0:T(8,128)S(1)} %get-tuple-element.21.refs_4_) | copy-start | bytes 786436

commit v4 on v3

--- a/solution.py
+++ b/solution.py
@@ -26,29 +26,33 @@
 
 
 def store(*refs):
-    sources, targets, sem = refs[:5], refs[5:10], refs[10]
+    sources, targets, held, load_sem, store_sem = refs[:5], refs[5:10], refs[10], refs[11], refs[12]
     layers = sources[0].shape[0]
     middle = layers // 2
     parts = (pl.ds(0, middle), pl.ds(middle, layers - middle))
-    copies = [
-        pltpu.make_async_copy(source.at[part], target.at[part], sem.at[k, side])
-        for k, (source, target) in enumerate(zip(sources, targets))
-        for side, part in enumerate(parts)
-    ]
-    for copy in copies:
-        copy.start()
-    for copy in copies:
+    loads, stores = [], []
+    for k, (source, target) in enumerate(zip(sources, targets)):
+        for side, part in enumerate(parts):
+            loads.append(pltpu.make_async_copy(source.at[part], held.at[k, part], load_sem.at[k, side]))
+            stores.append(pltpu.make_async_copy(held.at[k, part], target.at[part], store_sem.at[k, side]))
+    for copy in loads:
+        copy.start()
+    for load, copy in zip(loads, stores):
+        load.wait()
+        copy.start()
+    for copy in stores:
         copy.wait()
 
 
 def kernel(
     nx, ny,
     t_ref, d_hbm, e_hbm, vx_hbm, vy_hbm, vz_hbm,
-    dens_out, energy_out, nvx_out, nvy_out, nvz_out, limit_out,
+    dens_hbm, energy_hbm, nvx_hbm, nvy_hbm, nvz_hbm, limit_out,
+    dens_out, energy_out, nvx_out, nvy_out, nvz_out,
     d_s, e_s, xp, vy_s, vz_s, div_s, rate_s,
     a_send, a_lo, a_hi, lm, nvx_h, swept, m_send, m_lo, m_hi, o_send, o_lo, o_hi,
     top_s, top_x, top_y,
-    load_sem, send_sem, recv_sem, x_send, x_recv, y_send, y_recv,
+    load_sem, out_sem, send_sem, recv_sem, x_send, x_recv, y_send, y_recv,
 ):
     layers, rows, cols = d_s.shape
     ix, iy = lax.axis_index("gx"), lax.axis_index("gy")
@@ -158,6 +162,17 @@
     @pl.loop(2, layers - 2)
     def _(l):
         lagrange(l)
+
+    stores = []
+
+    def store_part(source, target, part=slice(None)):
+        copy = pltpu.make_async_copy(source.at[part], target.at[part], out_sem.at[len(stores)])
+        copy.start()
+        stores.append(copy)
+
+    store_part(nvx_out, nvx_hbm)
+    store_part(nvy_out, nvy_hbm)
+    store_part(nvz_out, nvz_hbm)
 
     def sweep_x(lower, upper):
         @pl.loop(0, rows // 8)
@@ -261,11 +276,17 @@
     top = lax.fori_loop(
         0, layers - 4, lambda i, top: finish(i + 2, i, m_lo, m_hi, top), jnp.zeros((rows, cols), jnp.float32)
     )
+    store_part(dens_out, dens_hbm, pl.ds(2, layers - 4))
+    store_part(energy_out, energy_hbm, pl.ds(2, layers - 4))
     for copy in outer:
         copy.wait()
     top = lax.fori_loop(
         0, 4, lambda i, top: finish(i + (i // 2) * (layers - 4), i, o_lo, o_hi, top), top
     )
+
+    for part in (pl.ds(0, 2), pl.ds(layers - 2, 2)):
+        store_part(dens_out, dens_hbm, part)
+        store_part(energy_out, energy_hbm, part)
 
     def reduced(value):
         return jnp.full((8, 128), jnp.max(value), jnp.float32)
@@ -291,6 +312,8 @@
     best = share(reduced(top), 0, top_x, nx, along_x, x_send, x_recv)
     best = share(best, 1, top_y, ny, along_y, y_send, y_recv)
     limit_out[0] = jnp.max(0.5 / best)
+    for copy in stores:
+        copy.wait()
 
 
 def local(nx, ny, density, energy, velocity_x, velocity_y, velocity_z, time_step):
@@ -303,10 +326,11 @@
     dma = pltpu.SemaphoreType.DMA
     results = pl.pallas_call(
         functools.partial(kernel, nx, ny),
-        out_shape=(full,) * 5 + (jax.ShapeDtypeStruct((1,), jnp.float32),),
+        out_shape=(pltpu.HBM(density.shape, jnp.float32),) * 5 + (jax.ShapeDtypeStruct((1,), jnp.float32),),
         in_specs=[pl.BlockSpec(memory_space=pltpu.SMEM)] + [pl.BlockSpec(memory_space=pltpu.HBM)] * 5,
-        out_specs=(pl.BlockSpec(memory_space=pltpu.VMEM),) * 5 + (pl.BlockSpec(memory_space=pltpu.SMEM),),
+        out_specs=(pl.BlockSpec(memory_space=pltpu.HBM),) * 5 + (pl.BlockSpec(memory_space=pltpu.SMEM),),
         scratch_shapes=[
+            *(vmem(layers, rows, cols) for _ in range(5)),
             vmem(layers, rows, cols), vmem(layers, rows, cols),
             vmem(layers + 2, 2, rows, cols),
             vmem(layers, rows, cols), vmem(layers, rows, cols),
@@ -318,7 +342,7 @@
             vmem(2, 5, layers - 4, cols), vmem(5, layers - 4, cols), vmem(5, layers - 4, cols),
             vmem(2, 5, 4, cols), vmem(5, 4, cols), vmem(5, 4, cols),
             vmem(2, 8, 128), vmem(nx - 1, 8, 128), vmem(ny - 1, 8, 128),
-            dma((5,)), dma((12,)), dma((12,)),
+            dma((5,)), dma((9,)), dma((12,)), dma((12,)),
             dma((nx - 1,)), dma((nx - 1,)), dma((ny - 1,)), dma((ny - 1,)),
         ],
         compiler_params=pltpu.CompilerParams(
@@ -328,10 +352,10 @@
     stored = pl.pallas_call(
         store,
         out_shape=(full,) * 5,
-        in_specs=[pl.BlockSpec(memory_space=pltpu.VMEM)] * 5,
+        in_specs=[pl.BlockSpec(memory_space=pltpu.HBM)] * 5,
         out_specs=(pl.BlockSpec(memory_space=pltpu.HBM),) * 5,
-        scratch_shapes=[dma((5, 2))],
-    )(*results[:5])
+        scratch_shapes=[vmem(5, layers, rows, cols), dma((5, 2)), dma((5, 2))],
+    )(*(pltpu.with_memory_space_constraint(f, pltpu.HBM) for f in results[:5]))
     return (*stored, results[5])
 
 

time: 35.9 us -> 32.3 us (0.90)
  local copies, waits for them, and re-layouts: 3.5 us -> 0 us
    unnamed x10 -> x0, local copies, waits for them, and re-layouts: 3.5 us -> none
where the time goes in v4:
time: 32.3 us; the launch traced here: 32.1 us
  Pallas kernels  29 us (90%)
  between operations  3.09 us (10%)
    pallas_call x1, Pallas kernels, local(): pl.pallas_call(functools.partial(kernel, nx, ny), out_shape=(pltpu.HBM(de...  26.8 us
    pallas_call x1, Pallas kernels, local(): pl.pallas_call(store, out_shape=(full,) * 5, in_specs=[pl.BlockSpec(memor...  2.21 us

profile of v4, /device:TPU:0, one launch (start us, length us, event | category | flops | bytes accessed | tf_op | source)
XLA Modules:
  0.0 32.1 jit_solution(12203822786718479914)
XLA Ops:
  1.3 26.8 %shard_map.109 = (f32[8,32,256]{2,1,0:T(8,128)}, f32[8,32,256]{2,1,0:T(8,128)}, f32[8,32,256]{2,1,0:T(8,128)}, f32[8,32,256]{2,1,0:T(8,128)}, f32[8,32,256]{2,1,0:T(8,128)}, /*index=5*/f32[1]{0:T(128)}) custom-call(f32[1]{0:T(128)S(6)} %copy.13.t_ref, f32[8,32,256]{2,1,0:T(8,128)} %d_hbm.1, f32[8,32,256]{2,1,0:T(8,128)} %e_hbm.1, f32[8,32,256]{2,1,0:T(8,128)} %vx_hbm.1, ...), custom_call_target="tpu_custom_call" | custom-call | tf_op jit(solution)/shard_map/pallas_call | solution.py:327
  28.0 2.2 %shard_map.110 = (f32[8,32,256]{2,1,0:T(8,128)}, f32[8,32,256]{2,1,0:T(8,128)}, f32[8,32,256]{2,1,0:T(8,128)}, f32[8,32,256]{2,1,0:T(8,128)}, f32[8,32,256]{2,1,0:T(8,128)}) custom-call(f32[8,32,256]{2,1,0:T(8,128)} %get-tuple-element.17.refs_0_, f32[8,32,256]{2,1,0:T(8,128)} %get-tuple-element.18.refs_1_, f32[8,32,256]{2,1,0:T(8,128)} %get-tuple-element.19.refs_2_, ...), custom_call_target="tpu_custom_call" | custom-call | tf_op jit(solution)/shard_map/pallas_call | solution.py:352
